TPU v7x, 256 devices: a whole 4x4x8 slice. The times are simulated.
256 devices in a mesh: hemi: 2 (over core), dev: 128 (over z, y, x).
Axes of the slice: x: 4, y: 4, z: 8, core: 2. Of those that a mesh axis runs over, the one named last changes fastest.
Arguments:
- spectrum: float32 [384, 512, 256], P(None, 'dev', 'hemi'), may hold values from 0.05 to 1
- wind_speed: float32 [512, 256], P('dev', 'hemi'), may hold values from 0.2 to 1
- src_counts: int32 [512, 256], P('dev', 'hemi'), may hold values from 1 to 3
- ocean_mask: int32 [512, 256], replicated, may hold values 0 or 1
- growth: float32 [384], replicated, may hold values from 0.1 to 0.6
- quadruplet: int32 [2, 384, 384], replicated, may hold values from 0 to 1, as said below
- courant: float32 [16], replicated, may hold values from 0.4 to 0.95
- freq_counts: int32 [16], replicated, may hold values from 1 to 4
Outputs:
- spectrum_next: float32 [384, 512, 256], P(None, 'dev', 'hemi')
Inputs may be any that keep to these rules, and one draw needn't show every extreme that they name: Each row of quadruplet[0] and of quadruplet[1] holds a single 1.
All inputs are finite; a program needn't handle non-finite values.
Results may differ from a plain program's by a relative error of at most 0.0003.
Values sent between devices are 32-bit elements; how exact they have to be, the bound alone decides.
No kernel may reach another device: no remote copies, remote signals or barrier semaphores. Data moves between devices by JAX's collectives and lax.ppermute only.
A program may use at most 64 MiB of HBM per device.

v0:
```python
import functools
import math

import jax
import jax.numpy as jnp
from jax import lax
from jax.experimental import pallas as pl
from jax.experimental.pallas import tpu as pltpu
from jax.sharding import PartitionSpec as P

ND = 24
NF = 16
K = ND * NF
LON = 4
LAT = 128
PTS = LON * LAT
SRC_MAX = 3
SPLIT = 2
GATHER_BLOCK = 128
SCATTER_BLOCK = 128
SUB_MAX = 4
HALF = K // 2
GROUP = 6 * NF
QUARTER = 6 * LON
coupling = 0.25
breaking = 0.5
spread = 0.7
MIB = 1024 * 1024


def direction(j, hemi):
    return lax.rem(18 + j + 12 * hemi, ND)


def split(value):
    high = value.astype(jnp.bfloat16)
    low = (value - high.astype(jnp.float32)).astype(jnp.bfloat16)
    return high, low


def source_terms(
    hemi, dev, ocean_ref, growth_ref, wind_ref, count_ref, quad_ref, spec_ref, waits, send,
    gather_m, scatter_m, energy, parts, paired, terms, moved, grow,
):
    nt = (((1,), (1,)), ((), ()))
    eye = (
        lax.broadcasted_iota(jnp.int32, (K, K), 0) == lax.broadcasted_iota(jnp.int32, (K, K), 1)
    ).astype(jnp.float32)
    eye_bf = eye.astype(jnp.bfloat16)
    waits["small"]()
    rest = jnp.broadcast_to(growth_ref[...].reshape(1, K), (LAT, K))
    column = None
    for _ in range(3):
        part = rest.astype(jnp.bfloat16)
        rest = rest - part.astype(jnp.float32)
        term = lax.dot_general(eye_bf, part, nt, preferred_element_type=jnp.float32)
        column = term if column is None else column + term
    grow[...] = column

    winds = []
    oceans = []
    counts = []
    for lon in range(LON):
        winds.append(wind_ref[lon:lon + 1, :])
        counts.append(count_ref[lon:lon + 1, :])
        row = ocean_ref[pl.ds(LON * lax.rem(dev, 2) + lon, 1), :].astype(jnp.float32)
        oceans.append(jnp.where(hemi == 0, row[:, :LAT], row[:, LAT:]))
    steps = [oceans[lon] / counts[lon].astype(jnp.float32) for lon in range(LON)]

    waits["quad"]()
    sides = []
    for side in range(2):
        rows = quad_ref[side * K:(side + 1) * K, :].astype(jnp.float32).astype(jnp.bfloat16)
        gather_m[side * K:(side + 1) * K, :K] = rows
        gather_m[side * K:(side + 1) * K, K:] = rows
        sides.append(rows)
    back = lax.dot_general(eye_bf, sides[0] + sides[1], nt, preferred_element_type=jnp.float32)
    back = (coupling * (back - 2.0 * eye)).astype(jnp.bfloat16)
    scatter_m[:, :K] = back
    scatter_m[:, K:] = back

    waits["spec"]()
    per = LON // SPLIT
    for part in range(SPLIT):
        for i in range(K // NF):
            for sub in range(per):
                lon = part * per + sub
                cols = slice(sub * LAT, (sub + 1) * LAT)
                value = spec_ref[pl.ds(i * NF * LON + lon, NF, stride=LON), :] * oceans[lon]
                energy[lon * K + i * NF:lon * K + (i + 1) * NF, :] = value
                high, low = split(value)
                parts[part, i * NF:(i + 1) * NF, cols] = high
                parts[part, K + i * NF:K + (i + 1) * NF, cols] = low

    def gather_rows(part, rows):
        def run():
            paired[part, rows, :] = jnp.dot(
                gather_m[rows, :], parts[part], preferred_element_type=jnp.float32
            )
        return run

    def scatter_rows(part, rows):
        def run():
            moved[part, rows, :] = jnp.dot(
                scatter_m[rows, :], terms[part], preferred_element_type=jnp.float32
            )
        return run

    def quad_rows(part, i):
        def run():
            at = slice(i * NF, (i + 1) * NF)
            below = slice(K + i * NF, K + (i + 1) * NF)
            for sub in range(per):
                lon = part * per + sub
                cols = slice(sub * LAT, (sub + 1) * LAT)
                value = energy[lon * K + i * NF:lon * K + (i + 1) * NF, :]
                plus = paired[part, at, cols]
                minus = paired[part, below, cols]
                term = value * (value * (plus + minus) - 2.0 * (plus * minus))
                high, low = split(term)
                terms[part, at, cols] = high
                terms[part, below, cols] = low
        return run

    def update_rows(part, i, cycle):
        def run():
            at = slice(i * NF, (i + 1) * NF)
            below = slice(K + i * NF, K + (i + 1) * NF)
            rate = grow[at, :]
            for sub in range(per):
                lon = part * per + sub
                cols = slice(sub * LAT, (sub + 1) * LAT)
                value = energy[lon * K + i * NF:lon * K + (i + 1) * NF, :]
                tendency = value * (rate * winds[lon] - breaking * value)
                tendency = tendency + moved[part, at, cols]
                value = jnp.where(cycle < counts[lon], value + steps[lon] * tendency, value)
                energy[lon * K + i * NF:lon * K + (i + 1) * NF, :] = value
                if cycle < SRC_MAX - 1:
                    high, low = split(value)
                    parts[part, at, cols] = high
                    parts[part, below, cols] = low
        return run

    def weave(dots, rows):
        per_dot = -(-len(rows) // max(len(dots), 1))
        for n in range(max(len(dots), 1)):
            for dot in dots[n:n + 1]:
                dot()
            for row in rows[n * per_dot:(n + 1) * per_dot]:
                row()

    def blocks(make, part, count, size):
        return [make(part, slice(n, n + size)) for n in range(0, count, size)]

    steps_of = K // NF
    weave(blocks(gather_rows, 0, 2 * K, GATHER_BLOCK), [])
    for cycle in range(SRC_MAX):
        weave(blocks(gather_rows, 1, 2 * K, GATHER_BLOCK), [quad_rows(0, i) for i in range(steps_of)])
        weave(blocks(scatter_rows, 0, K, SCATTER_BLOCK), [quad_rows(1, i) for i in range(steps_of)])
        weave(blocks(scatter_rows, 1, K, SCATTER_BLOCK), [update_rows(0, i, cycle) for i in range(steps_of)])
        if cycle < SRC_MAX - 1:
            weave(blocks(gather_rows, 0, 2 * K, GATHER_BLOCK), [update_rows(1, i, cycle) for i in range(steps_of)])
        else:
            for lon in range(per):
                send(lon)
            weave([], [update_rows(1, i, cycle) for i in range(steps_of)])
            for lon in range(per, LON):
                send(lon)


def source_kernel(
    spec, wind, count, growth, quad, ocean, east, west,
    spec_v, wind_v, count_v, growth_v, quad_v, ocean_v, first_v, second_v, sems, *work,
):
    hemi = lax.axis_index("hemi")
    dev = lax.axis_index("dev")
    block = pl.multiple_of(dev // 2 * 8, 8)
    small = [
        pltpu.make_async_copy(growth, growth_v, sems.at[2]),
        pltpu.make_async_copy(wind, wind_v, sems.at[3]),
        pltpu.make_async_copy(count, count_v, sems.at[4]),
        pltpu.make_async_copy(ocean.at[pl.ds(block, 8), :], ocean_v, sems.at[5]),
    ]
    large = {
        "quad": pltpu.make_async_copy(quad, quad_v, sems.at[0]),
        "spec": pltpu.make_async_copy(spec, spec_v, sems.at[1]),
    }
    large["quad"].start()
    for copy in small:
        copy.start()
    large["spec"].start()

    def wait_small():
        for copy in small:
            copy.wait()

    waits = {"small": wait_small, "quad": large["quad"].wait, "spec": large["spec"].wait}
    outs = []

    def send(lon):
        for slot, source in enumerate((first_v, second_v)):
            forward = hemi if slot == 0 else 1 - hemi
            n = lon + forward * (LON - 1 - 2 * lon)
            rows = pl.ds(pl.multiple_of(n * HALF, HALF), HALF)
            for jj in range(12):
                d = direction(jj + 12 * slot, hemi)
                source[lon, jj * NF:(jj + 1) * NF, :] = work[2][pl.ds(lon * K + d, NF, stride=ND), :]
            for side in range(2):
                copy = pltpu.make_async_copy(
                    source.at[lon], (east, west)[slot ^ side].at[rows, :], sems.at[6 + 2 * lon + slot]
                )
                pl.when(hemi == side)(copy.start)
            outs.append(copy)

    source_terms(
        hemi, dev, ocean_v, growth_v, wind_v, count_v, quad_v, spec_v, waits, send, *work,
    )
    for copy in outs:
        copy.wait()


BATCH = (6, 6)


def fine(value, active):
    return value if active is None else jnp.where(active, value, 0.0)


def total(*terms):
    terms = [term for term in terms if term is not None]
    if not terms:
        return None
    out = terms[0]
    for term in terms[1:]:
        out = out + term
    return out


def times(rate, value):
    return None if value is None else rate * value


def advance(slot, hemi, courant_ref, times_ref, masks_ref, load, store, which=(1, 0)):
    forward = hemi if slot == 0 else 1 - hemi
    lanes = slice(hemi * LAT, (hemi + 1) * LAT)
    far_lanes = slice((1 - hemi) * LAT, (2 - hemi) * LAT)
    masks = []
    far_masks = []
    for n in range(-LON, LON):
        at = LON + (n if forward == 0 else LON - 1 - n)
        masks.append(jnp.broadcast_to(masks_ref[at:at + 1, lanes], (8, LAT)))
        far_masks.append(jnp.broadcast_to(masks_ref[at:at + 1, far_lanes], (8, LAT)))
    lane = lax.broadcasted_iota(jnp.int32, (8, LAT), 1)
    row8 = lax.broadcasted_iota(jnp.int32, (8, LAT), 0)
    rates = []
    for half in range(2):
        courant = jnp.zeros((8, LAT), jnp.float32)
        count = jnp.zeros((8, LAT), jnp.int32)
        for r in range(8):
            courant = jnp.where(row8 == r, courant_ref[half * 8 + r], courant)
            count = jnp.where(row8 == r, times_ref[half * 8 + r], count)
        rates.append((spread * courant, [None] + [count > t for t in range(1, SUB_MAX)]))
    for toward in which:
        up = hemi if toward == 0 else 1 - hemi
        shift = 1 if up else LAT - 1
        edge = lane == (0 if up else LAT - 1)
        batch = BATCH[toward]
        for half in range(2):
            speed, active = rates[half]
            for first in range(0, 6, batch):
                groups = []
                for i in range(first, first + batch):
                    jj = i + (6 * toward if slot == 0 else 6 * (1 - toward))
                    angle = 2.0 * math.pi * ((18 + jj + 12 * slot) % ND + 0.5) / ND
                    cx = speed * abs(math.cos(angle))
                    cy = speed * abs(math.sin(angle))
                    base = jj * NF + half * 8
                    cross = i * NF + half * 8
                    groups.append((base, cross, cx, cy, 1.0 - cx - cy, load(base), [None] * (2 * LON)))
                for t in range(SUB_MAX):
                    for n in range(2 * LON - 1, t, -1):
                        for base, cross, cx, cy, stay, level, far in groups:
                            rolled = None if level[n] is None else pltpu.roll(level[n], shift, 1)
                            south = None if rolled is None else jnp.where(edge, 0.0, rolled)
                            value = total(times(stay, level[n]), times(cx, level[n - 1]), times(cy, south))
                            if toward:
                                inflow = None
                                if far[n] is not None:
                                    inflow = jnp.where(edge, rolled, pltpu.roll(far[n], shift, 1))
                                elif rolled is not None:
                                    inflow = jnp.where(edge, rolled, 0.0)
                                other = total(times(stay, far[n]), times(cx, far[n - 1]), times(cy, inflow))
                                if other is not None:
                                    other = far_masks[n] * other
                                    if t:
                                        old = 0.0 if far[n] is None else far[n]
                                        other = jnp.where(active[t], other, old)
                                    far[n] = other
                            if value is not None:
                                value = masks[n] * value
                                if t:
                                    old = 0.0 if level[n] is None else level[n]
                                    value = jnp.where(active[t], value, old)
                                level[n] = value
                for base, cross, cx, cy, stay, level, far in groups:
                    store(base, level[LON:], cross, far[LON:] if toward else None)


def own_rows(base, n):
    return slice(n * HALF + base, n * HALF + base + 8)


def cross_rows(cross, n):
    return slice(n * GROUP + cross, n * GROUP + cross + 8)


def own_kernel(
    courant_ref, times_ref, ocean, east, west, out0, out1, cross0, cross1, masks,
    first_v, second_v, ocean_v, sems,
):
    hemi = lax.axis_index("hemi")
    dev = lax.axis_index("dev")
    n_dev = lax.axis_size("dev")
    start = lax.rem(dev + n_dev - 1, n_dev)
    block = start // 2
    blocks = n_dev * LON // 8
    copies = []
    for i in range(2):
        at = pl.multiple_of(lax.rem(block + i, blocks) * 8, 8)
        copies.append(
            pltpu.make_async_copy(
                ocean.at[pl.ds(at, 8), :], ocean_v.at[pl.ds(8 * i, 8), :], sems.at[i]
            )
        )
        copies[i].start()

    for side in range(2):

        @pl.when(hemi == side)
        def _(side=side):
            pltpu.make_async_copy((east, west)[side], first_v, sems.at[2]).start()
            pltpu.make_async_copy((west, east)[side], second_v, sems.at[3]).start()

    copies.append(pltpu.make_async_copy(east, first_v, sems.at[2]))
    copies.append(pltpu.make_async_copy(west, second_v, sems.at[3]))
    for copy in copies:
        copy.wait()
    offset = start * LON - block * 8
    for i in range(3 * LON):
        masks[i:i + 1, :] = ocean_v[pl.ds(offset + i, 1), :].astype(jnp.float32)

    def run(slot, side, own_ref, out_ref, cross_ref):
        def load(base):
            return [None] * LON + [own_ref[own_rows(base, n), :] for n in range(LON)]

        def store(base, level, cross, far):
            for n in range(LON):
                out_ref[own_rows(base, n), :] = level[n]
                if far is not None:
                    cross_ref[cross_rows(cross, n), :] = far[n]

        advance(slot, side, courant_ref, times_ref, masks, load, store)

    for side in range(2):

        @pl.when(hemi == side)
        def _(side=side):
            run(0, side, first_v, out0, cross0)
            run(1, side, second_v, out1, cross1)


def halo_load(halo_ref):
    def load(base):
        return [halo_ref[own_rows(base, n), :] for n in range(LON)] + [None] * LON

    return load


def stage_rows(slot, hemi, base, n):
    i = base // NF % 6
    forward = hemi if slot == 0 else 1 - hemi
    lon = LON - 1 - n if forward else n
    return pl.ds((base % NF) * QUARTER + i * LON + lon, 8, stride=QUARTER)


def quarter_copy(slot, toward, stage, out, sem):
    hemi = lax.axis_index("hemi")
    part = slot if toward else 1 - slot
    at = pl.multiple_of(2 * QUARTER * (hemi if toward else 1 - hemi) + QUARTER * part, 8)
    return pltpu.make_async_copy(
        stage.reshape(NF, QUARTER, LAT), out.at[:, pl.ds(at, QUARTER), :], sem
    )


def group_bases(slot, toward):
    first = 6 * toward if slot == 0 else 6 * (1 - toward)
    return [(i * NF + half * 8 + first * NF, i * NF + half * 8) for i in range(6) for half in range(2)]


def add_halo(slot, toward, side, rates, load, acc, stage, cross_in=None, cross_out=None):
    def store(base, level, cross, far):
        for n in range(LON):
            rows = stage_rows(slot, side, base, n)
            stage[rows, :] = acc[own_rows(base, n), :] + level[n]
            if far is not None:
                value = cross_in[cross_rows(cross, n), :]
                cross_out[cross_rows(cross, n), :] = total(value, far[n])

    advance(slot, side, *rates, load, store, (toward,))


def toward_kernel(courant_ref, times_ref, masks_ref, east, west, acc0, acc1, cross0, cross1, _,
                  ready0, ready1, cross_out):
    rates = (courant_ref, times_ref, masks_ref)
    for side in range(2):

        @pl.when(lax.axis_index("hemi") == side)
        def _(side=side):
            halo0, halo1 = (east, west) if side == 0 else (west, east)
            add_halo(0, 1, side, rates, halo_load(halo0), acc0, ready0, cross0, cross_out.at[0])
            add_halo(1, 1, side, rates, halo_load(halo1), acc1, ready1, cross1, cross_out.at[1])


def mark_kernel(*refs):
    refs[-1][...] = jnp.zeros((8, LAT), jnp.float32)


def away_kernel(courant_ref, times_ref, masks_ref, east, west, acc0, acc1, ready0, ready1,
                stage0, stage1, out, sems):
    copies = [quarter_copy(0, 1, ready0, out, sems.at[0]), quarter_copy(1, 1, ready1, out, sems.at[1])]
    for copy in copies:
        copy.start()
    rates = (courant_ref, times_ref, masks_ref)
    for side in range(2):

        @pl.when(lax.axis_index("hemi") == side)
        def _(side=side):
            halo0, halo1 = (east, west) if side == 0 else (west, east)
            add_halo(0, 0, side, rates, halo_load(halo0), acc0, stage0)
            add_halo(1, 0, side, rates, halo_load(halo1), acc1, stage1)

    for copy in copies:
        copy.wait()


def join_kernel(stage0, stage1, cross, _, out, ready0, ready1, sems):
    copies = []
    for slot, stage, ready in ((0, stage0, ready0), (1, stage1, ready1)):
        for side in range(2):

            @pl.when(lax.axis_index("hemi") == side)
            def _(side=side):
                first = 6 * slot * NF
                for i in range(6):
                    for half in range(2):
                        at = i * NF + half * 8
                        for n in range(LON):
                            rows = stage_rows(slot, side, first + at, n)
                            ready[rows, :] = stage[rows, :] + cross[1 - slot, cross_rows(at, n), :]

        copies.append(quarter_copy(slot, 0, ready, out, sems.at[slot]))
        copies[slot].start()
    for copy in copies:
        copy.wait()


SMEM = pl.BlockSpec(memory_space=pltpu.SMEM)
VMEM = pl.BlockSpec(memory_space=pltpu.VMEM)
HBM = pl.BlockSpec(memory_space=pltpu.HBM)


def params(mib=40):
    return pltpu.CompilerParams(vmem_limit_bytes=int(mib * MIB))


def cost(flops):
    return pl.CostEstimate(flops=int(flops), bytes_accessed=1000, transcendentals=0)


SOURCE_SCRATCH = [
    pltpu.VMEM((K * LON, LAT), jnp.float32),
    pltpu.VMEM((LON, LAT), jnp.float32),
    pltpu.VMEM((LON, LAT), jnp.int32),
    pltpu.VMEM((K,), jnp.float32),
    pltpu.VMEM((2 * K, K), jnp.int32),
    pltpu.VMEM((8, 2 * LAT), jnp.int32),
    pltpu.VMEM((LON, HALF, LAT), jnp.float32),
    pltpu.VMEM((LON, HALF, LAT), jnp.float32),
    pltpu.SemaphoreType.DMA((6 + 2 * LON,)),
    pltpu.VMEM((2 * K, 2 * K), jnp.bfloat16),
    pltpu.VMEM((K, 2 * K), jnp.bfloat16),
    pltpu.VMEM((K * LON, LAT), jnp.float32),
    pltpu.VMEM((SPLIT, 2 * K, PTS // SPLIT), jnp.bfloat16),
    pltpu.VMEM((SPLIT, 2 * K, PTS // SPLIT), jnp.float32),
    pltpu.VMEM((SPLIT, 2 * K, PTS // SPLIT), jnp.bfloat16),
    pltpu.VMEM((SPLIT, K, PTS // SPLIT), jnp.float32),
    pltpu.VMEM((K, LAT), jnp.float32),
]


def local(spectrum, wind_speed, src_counts, ocean_mask, growth, quadruplet, courant, freq_counts):
    n_dev = lax.axis_size("dev")
    half_shape = jax.ShapeDtypeStruct((LON * HALF, LAT), jnp.float32)
    cross_shape = jax.ShapeDtypeStruct((LON * GROUP, LAT), jnp.float32)
    mask_shape = jax.ShapeDtypeStruct((3 * LON, 2 * LAT), jnp.float32)
    out_shape = jax.ShapeDtypeStruct((NF, ND * LON, LAT), jnp.float32)
    given = (
        spectrum.reshape(K * LON, LAT), wind_speed, src_counts, growth,
        quadruplet.reshape(2 * K, K), ocean_mask,
    )

    east, west = pl.pallas_call(
        source_kernel,
        out_shape=(half_shape, half_shape),
        in_specs=[HBM] * 6,
        out_specs=(HBM, HBM),
        scratch_shapes=SOURCE_SCRATCH,
        compiler_params=params(56),
        cost_estimate=cost(6e9),
    )(*given)

    ring = range(n_dev)
    halo_east = lax.ppermute(east, "dev", [(i, (i + 1) % n_dev) for i in ring])
    halo_west = lax.ppermute(west, "dev", [(i, (i - 1) % n_dev) for i in ring])

    out0, out1, cross0, cross1, masks = pl.pallas_call(
        own_kernel,
        out_shape=(half_shape, half_shape, cross_shape, cross_shape, mask_shape),
        in_specs=[SMEM] * 2 + [HBM] * 3,
        out_specs=(VMEM,) * 5,
        scratch_shapes=[
            pltpu.VMEM((LON * HALF, LAT), jnp.float32),
            pltpu.VMEM((LON * HALF, LAT), jnp.float32),
            pltpu.VMEM((16, 2 * LAT), jnp.int32),
            pltpu.SemaphoreType.DMA((4,)),
        ],
        compiler_params=params(52.6),
        cost_estimate=cost(3e9),
    )(courant, freq_counts, ocean_mask, east, west)
    rates = (courant, freq_counts, masks)
    quarter_shape = jax.ShapeDtypeStruct((NF * QUARTER, LAT), jnp.float32)

    def tail(kernel, outs, count, *operands, **more):
        return pl.pallas_call(
            kernel,
            out_shape=outs,
            in_specs=[SMEM] * 2 + [VMEM] * (1 + count),
            compiler_params=params(),
            cost_estimate=cost(1e9),
            **more,
        )(*rates, *operands)

    def mark(*values):
        return pl.pallas_call(
            mark_kernel,
            out_shape=jax.ShapeDtypeStruct((8, LAT), jnp.float32),
            in_specs=[VMEM] * len(values),
            out_specs=VMEM,
            compiler_params=params(),
            cost_estimate=cost(1e8),
        )(*values)

    order = mark(halo_east, out0)
    both_shape = jax.ShapeDtypeStruct((2, LON * GROUP, LAT), jnp.float32)
    halos = (halo_east, halo_west, out0, out1)
    ready0, ready1, cross = tail(
        toward_kernel, (quarter_shape, quarter_shape, both_shape), 7, *halos, cross0, cross1, order,
        out_specs=(VMEM,) * 3,
    )
    cross = lax.ppermute(cross, "hemi", [(0, 1), (1, 0)])
    stage0, stage1, out = tail(
        away_kernel, (quarter_shape, quarter_shape, out_shape), 6, *halos, ready0, ready1,
        out_specs=(VMEM, VMEM, HBM), scratch_shapes=[pltpu.SemaphoreType.DMA((2,))],
    )
    out = pl.pallas_call(
        join_kernel,
        out_shape=out_shape,
        in_specs=[VMEM] * 3 + [HBM],
        out_specs=HBM,
        scratch_shapes=[
            pltpu.VMEM((NF * QUARTER, LAT), jnp.float32),
            pltpu.VMEM((NF * QUARTER, LAT), jnp.float32),
            pltpu.SemaphoreType.DMA((2,)),
        ],
        input_output_aliases={3: 0},
        compiler_params=params(),
    )(stage0, stage1, cross, out)
    return out.reshape(K, LON, LAT)


def solution(mesh):
    return jax.shard_map(
        local,
        mesh=mesh,
        in_specs=(
            P(None, "dev", "hemi"),
            P("dev", "hemi"),
            P("dev", "hemi"),
            P(),
            P(),
            P(),
            P(),
            P(),
        ),
        out_specs=P(None, "dev", "hemi"),
        check_vma=False,
    )
```

profile of v0, /device:TPU:1, one launch (start us, length us, event | category | flops | bytes accessed | tf_op | source)
XLA Modules:
  0.0 31.3 jit_solution(8768840459418578670)
XLA Ops:
  0.0 0.0 copy-start
  0.0 0.0 copy-start.1
  0.0 6.3 %shard_map.82 = (f32[768,128]{1,0:T(8,128)}, f32[768,128]{1,0:T(8,128)}) custom-call(f32[1536,128]{1,0:T(8,128)} %bitcast.4, f32[4,128]{1,0:T(4,128)} %wind.1, s32[4,128]{1,0:T(4,128)} %count.1, f32[384]{0:T(512)} %growth.1, s32[768,384]{1,0:T(8,128)} %bitcast.3, s32[512,256]{1,0:T(8,128)} %ocean.3), custom_call_target="tpu_custom_call" | custom-call | flops 6000000000 | bytes 1000 | tf_op jit(solution)/shard_map/pallas_call | solution.py:512
  6.3 2.1 %collective-permute-start = (f32[768,128]{1,0:T(8,128)}, f32[768,128]{1,0:T(8,128)S(1)}, u32[]{:S(2)}, u32[]{:S(2)}) collective-permute-start(f32[768,128]{1,0:T(8,128)} %get-tuple-element.18.east), channel_id=1, source_target_pairs={{0,1},{1,2},{2,3},{3,4},{4,5},{5,6},{6,7},{7,8},{8,9},{9,10},{10,1... | collective-permute-start | bytes 1179656 | tf_op jit(solution)/shard_map/ppermute | solution.py:523
  8.4 9.1 %collective-permute-start.1 = (f32[768,128]{1,0:T(8,128)}, f32[768,128]{1,0:T(8,128)S(1)}, u32[]{:S(2)}, u32[]{:S(2)}) collective-permute-start(f32[768,128]{1,0:T(8,128)} %get-tuple-element.19.west), channel_id=1, source_target_pairs={{0,127},{1,0},{2,1},{3,2},{4,3},{5,4},{6,5},{7,6},{8,7},{9,8},{10,... | collective-permute-start | bytes 1179656 | tf_op jit(solution)/shard_map/ppermute | solution.py:524
  17.5 0.0 copy-done
  17.5 0.0 copy-done.1
  17.5 3.7 %shard_map.83 = (f32[768,128]{1,0:T(8,128)S(1)}, f32[768,128]{1,0:T(8,128)S(1)}, f32[384,128]{1,0:T(8,128)S(1)}, f32[384,128]{1,0:T(8,128)S(1)}, f32[12,256]{1,0:T(8,128)S(1)}) custom-call(f32[16]{0:T(128)S(1)} %copy-done, s32[16]{0:T(128)S(1)} %copy-done.1, s32[512,256]{1,0:T(8,128)} %ocean.3, f32[768,128]{1,0:T(8,128)} %get-tuple-element.18.east, ...), custom_call_target="tpu_custom_call" | custom-call | flops 3000000000 | bytes 1000 | tf_op jit(solution)/shard_map/pallas_call | solution.py:526
  21.1 5.3 %collective-permute-done.refs_0_.east = f32[768,128]{1,0:T(8,128)S(1)} collective-permute-done((f32[768,128]{1,0:T(8,128)}, f32[768,128]{1,0:T(8,128)S(1)}, u32[]{:S(2)}, u32[]{:S(2)}) %collective-permute-start) | collective-permute-done | bytes 393248 | tf_op jit(solution)/shard_map/ppermute | solution.py:523
  26.5 0.0 collective-permute-done.1.west
  26.5 1.4 %shard_map.85 = (f32[384,128]{1,0:T(8,128)S(1)}, f32[384,128]{1,0:T(8,128)S(1)}, f32[2,384,128]{2,1,0:T(8,128)S(1)}) custom-call(f32[16]{0:T(128)S(1)} %copy-done, s32[16]{0:T(128)S(1)} %copy-done.1, f32[12,256]{1,0:T(8,128)S(1)} %get-tuple-element.20.masks_ref, f32[768,128]{1,0:T(8,128)S(1)} %collective-permute-done.refs_0_.east, ...), custom_call_target="tpu_custom_call" | custom-call | flops 1000000000 | bytes 1000 | tf_op jit(solution)/shard_map/pallas_call | solution.py:544
  27.8 1.3 %collective-permute-start.2 = (f32[2,384,128]{2,1,0:T(8,128)S(1)}, f32[2,384,128]{2,1,0:T(8,128)S(1)}, u32[]{:S(2)}, u32[]{:S(2)}) collective-permute-start(f32[2,384,128]{2,1,0:T(8,128)S(1)} %get-tuple-element.29), channel_id=1, source_target_pairs={{0,128},{128,0},{1,129},{129,1},{2,130},{130,2},{3,131},{131,3},{4... | collective-permute-start | bytes 1179656 | tf_op jit(solution)/shard_map/ppermute | solution.py:570
  29.1 1.3 %shard_map.86 = (f32[384,128]{1,0:T(8,128)S(1)}, f32[384,128]{1,0:T(8,128)S(1)}, f32[16,96,128]{2,1,0:T(8,128)}) custom-call(f32[16]{0:T(128)S(1)} %copy-done, s32[16]{0:T(128)S(1)} %copy-done.1, f32[12,256]{1,0:T(8,128)S(1)} %get-tuple-element.20.masks_ref, f32[768,128]{1,0:T(8,128)S(1)} %collective-permute-done.refs_0_.east, ...), custom_call_target="tpu_custom_call" | custom-call | flops 1000000000 | bytes 1000 | tf_op jit(solution)/shard_map/pallas_call | solution.py:544
  30.5 0.0 collective-permute-done.2.cross
  30.5 0.8 %shard_map.87 = f32[16,96,128]{2,1,0:T(8,128)} custom-call(f32[384,128]{1,0:T(8,128)S(1)} %get-tuple-element.27.stage0, f32[384,128]{1,0:T(8,128)S(1)} %get-tuple-element.28.stage1, f32[2,384,128]{2,1,0:T(8,128)S(1)} %collective-permute-done.2.cross, f32[16,96,128]{2,1,0:T(8,128)} %get-tuple-element.30._), custom_call_target="tpu_custom_call", output_to_operand_aliasing={{}: (3, {})} | custom-call | tf_op jit(solution)/shard_map/pallas_call | solution.py:575
  (1 shorter events, 0.0 us)
Async XLA Ops:
  0.0 17.5 %copy-start = (f32[16]{0:T(128)S(1)}, f32[16]{0:T(128)}, u32[]{:S(2)}) copy-start(f32[16]{0:T(128)} %courant_ref.5) | copy-start | bytes 196
  0.0 17.5 %copy-start.1 = (s32[16]{0:T(128)S(1)}, s32[16]{0:T(128)}, u32[]{:S(2)}) copy-start(s32[16]{0:T(128)} %times_ref.5) | copy-start | bytes 196
  6.3 20.2 %collective-permute-start = (f32[768,128]{1,0:T(8,128)}, f32[768,128]{1,0:T(8,128)S(1)}, u32[]{:S(2)}, u32[]{:S(2)}) collective-permute-start(f32[768,128]{1,0:T(8,128)} %get-tuple-element.18.east), channel_id=1, source_target_pairs={{0,1},{1,2},{2,3},{3,4},{4,5},{5,6},{6,7},{7,8},{8,9},{9,10},{10,1... | collective-permute-start | bytes 1179656 | tf_op jit(solution)/shard_map/ppermute | solution.py:523
  8.4 18.1 %collective-permute-start.1 = (f32[768,128]{1,0:T(8,128)}, f32[768,128]{1,0:T(8,128)S(1)}, u32[]{:S(2)}, u32[]{:S(2)}) collective-permute-start(f32[768,128]{1,0:T(8,128)} %get-tuple-element.19.west), channel_id=1, source_target_pairs={{0,127},{1,0},{2,1},{3,2},{4,3},{5,4},{6,5},{7,6},{8,7},{9,8},{10,... | collective-permute-start | bytes 1179656 | tf_op jit(solution)/shard_map/ppermute | solution.py:524
  27.8 2.7 %collective-permute-start.2 = (f32[2,384,128]{2,1,0:T(8,128)S(1)}, f32[2,384,128]{2,1,0:T(8,128)S(1)}, u32[]{:S(2)}, u32[]{:S(2)}) collective-permute-start(f32[2,384,128]{2,1,0:T(8,128)S(1)} %get-tuple-element.29), channel_id=1, source_target_pairs={{0,128},{128,0},{1,129},{129,1},{2,130},{130,2},{3,131},{131,3},{4... | collective-permute-start | bytes 1179656 | tf_op jit(solution)/shard_map/ppermute | solution.py:570
where the time goes:
time: 31.4 us; the launch traced here: 31.3 us
  Pallas kernels  13.4 us (43%)
  starting transfers between devices  12.5 us (40%)
  waiting for transfers between devices  5.34 us (17%)
    ppermute x1, starting transfers between devices, local(): halo_west = lax.ppermute(west, 'dev', [(i, (i - 1) % n_dev) for i in ring])  9.09 us
    pallas_call x1, Pallas kernels, local(): pl.pallas_call(source_kernel, out_shape=(half_shape, half_shape), in_spec...  6.25 us
    ppermute x1, waiting for transfers between devices, local(): halo_east = lax.ppermute(east, 'dev', [(i, (i + 1) % n_dev) for i in ring])  5.3 us
    pallas_call x1, Pallas kernels, local(): pl.pallas_call(own_kernel, out_shape=(half_shape, half_shape, cross_shape...  3.65 us
    pallas_call x2, Pallas kernels, tail(): pl.pallas_call(kernel, out_shape=outs, in_specs=[SMEM] * 2 + [VMEM] * (1...  2.67 us
    ppermute x1, starting transfers between devices, local(): halo_east = lax.ppermute(east, 'dev', [(i, (i + 1) % n_dev) for i in ring])  2.12 us
    ppermute x1, starting transfers between devices, local(): cross = lax.ppermute(cross, 'hemi', [(0, 1), (1, 0)])  1.31 us
    pallas_call x1, Pallas kernels, local(): pl.pallas_call(join_kernel, out_shape=out_shape, in_specs=[VMEM] * 3 + [H...  0.81 us
  transfers between devices with their start and end apart: 3, of which 1 were waited for; matrix products, arithmetic and copies ran while one was open for 0% of the time, Pallas kernels for 16%

commit v1 on v0

--- a/solution.py
+++ b/solution.py
@@ -219,7 +219,7 @@
         copy.wait()
 
 
-BATCH = (6, 6)
+BATCH = (12, 6)
 
 
 def fine(value, active):
@@ -265,45 +265,45 @@
         shift = 1 if up else LAT - 1
         edge = lane == (0 if up else LAT - 1)
         batch = BATCH[toward]
-        for half in range(2):
-            speed, active = rates[half]
-            for first in range(0, 6, batch):
-                groups = []
-                for i in range(first, first + batch):
-                    jj = i + (6 * toward if slot == 0 else 6 * (1 - toward))
-                    angle = 2.0 * math.pi * ((18 + jj + 12 * slot) % ND + 0.5) / ND
-                    cx = speed * abs(math.cos(angle))
-                    cy = speed * abs(math.sin(angle))
-                    base = jj * NF + half * 8
-                    cross = i * NF + half * 8
-                    groups.append((base, cross, cx, cy, 1.0 - cx - cy, load(base), [None] * (2 * LON)))
-                for t in range(SUB_MAX):
-                    for n in range(2 * LON - 1, t, -1):
-                        for base, cross, cx, cy, stay, level, far in groups:
-                            rolled = None if level[n] is None else pltpu.roll(level[n], shift, 1)
-                            south = None if rolled is None else jnp.where(edge, 0.0, rolled)
-                            value = total(times(stay, level[n]), times(cx, level[n - 1]), times(cy, south))
-                            if toward:
-                                inflow = None
-                                if far[n] is not None:
-                                    inflow = jnp.where(edge, rolled, pltpu.roll(far[n], shift, 1))
-                                elif rolled is not None:
-                                    inflow = jnp.where(edge, rolled, 0.0)
-                                other = total(times(stay, far[n]), times(cx, far[n - 1]), times(cy, inflow))
-                                if other is not None:
-                                    other = far_masks[n] * other
-                                    if t:
-                                        old = 0.0 if far[n] is None else far[n]
-                                        other = jnp.where(active[t], other, old)
-                                    far[n] = other
-                            if value is not None:
-                                value = masks[n] * value
+        both = [(half, i) for half in range(2) for i in range(6)]
+        for first in range(0, 12, batch):
+            groups = []
+            for half, i in both[first:first + batch]:
+                speed, active = rates[half]
+                jj = i + (6 * toward if slot == 0 else 6 * (1 - toward))
+                angle = 2.0 * math.pi * ((18 + jj + 12 * slot) % ND + 0.5) / ND
+                cx = speed * abs(math.cos(angle))
+                cy = speed * abs(math.sin(angle))
+                base = jj * NF + half * 8
+                cross = i * NF + half * 8
+                groups.append((base, cross, cx, cy, 1.0 - cx - cy, load(base), [None] * (2 * LON), active))
+            for t in range(SUB_MAX):
+                for n in range(2 * LON - 1, t, -1):
+                    for base, cross, cx, cy, stay, level, far, active in groups:
+                        rolled = None if level[n] is None else pltpu.roll(level[n], shift, 1)
+                        south = None if rolled is None else jnp.where(edge, 0.0, rolled)
+                        value = total(times(stay, level[n]), times(cx, level[n - 1]), times(cy, south))
+                        if toward:
+                            inflow = None
+                            if far[n] is not None:
+                                inflow = jnp.where(edge, rolled, pltpu.roll(far[n], shift, 1))
+                            elif rolled is not None:
+                                inflow = jnp.where(edge, rolled, 0.0)
+                            other = total(times(stay, far[n]), times(cx, far[n - 1]), times(cy, inflow))
+                            if other is not None:
+                                other = far_masks[n] * other
                                 if t:
-                                    old = 0.0 if level[n] is None else level[n]
-                                    value = jnp.where(active[t], value, old)
-                                level[n] = value
-                for base, cross, cx, cy, stay, level, far in groups:
-                    store(base, level[LON:], cross, far[LON:] if toward else None)
+                                    old = 0.0 if far[n] is None else far[n]
+                                    other = jnp.where(active[t], other, old)
+                                far[n] = other
+                        if value is not None:
+                            value = masks[n] * value
+                            if t:
+                                old = 0.0 if level[n] is None else level[n]
+                                value = jnp.where(active[t], value, old)
+                            level[n] = value
+            for base, cross, cx, cy, stay, level, far, active in groups:
+                store(base, level[LON:], cross, far[LON:] if toward else None)
 
 
 def own_rows(base, n):

time: 31.4 us -> 31.4 us (level)
  transfers between devices with their start and end apart: 3 -> 3, of which waited for: 1 -> 1; matrix products, arithmetic and copies ran while one was open for 0% -> 0% of each run, Pallas kernels for 16% -> 15%
where the time goes in v1:
time: 31.4 us; the launch traced here: 31.3 us
  Pallas kernels  13.1 us (42%)
  starting transfers between devices  12.5 us (40%)
  waiting for transfers between devices  5.62 us (18%)
    ppermute x1, starting transfers between devices, local(): halo_west = lax.ppermute(west, 'dev', [(i, (i - 1) % n_dev) for i in ring])  9.09 us
    pallas_call x1, Pallas kernels, local(): pl.pallas_call(source_kernel, out_shape=(half_shape, half_shape), in_spec...  6.25 us
    ppermute x1, waiting for transfers between devices, local(): halo_east = lax.ppermute(east, 'dev', [(i, (i + 1) % n_dev) for i in ring])  5.58 us
    pallas_call x1, Pallas kernels, local(): pl.pallas_call(own_kernel, out_shape=(half_shape, half_shape, cross_shape...  3.37 us
    pallas_call x2, Pallas kernels, tail(): pl.pallas_call(kernel, out_shape=outs, in_specs=[SMEM] * 2 + [VMEM] * (1...  2.67 us
    ppermute x1, starting transfers between devices, local(): halo_east = lax.ppermute(east, 'dev', [(i, (i + 1) % n_dev) for i in ring])  2.12 us
    ppermute x1, starting transfers between devices, local(): cross = lax.ppermute(cross, 'hemi', [(0, 1), (1, 0)])  1.31 us
    pallas_call x1, Pallas kernels, local(): pl.pallas_call(join_kernel, out_shape=out_shape, in_specs=[VMEM] * 3 + [H...  0.81 us
  transfers between devices with their start and end apart: 3, of which 1 were waited for; matrix products, arithmetic and copies ran while one was open for 0% of the time, Pallas kernels for 15%

profile of v1, /device:TPU:1, one launch (start us, length us, event | category | flops | bytes accessed | tf_op | source)
XLA Modules:
  0.0 31.3 jit_solution(14517059480761701438)
XLA Ops:
  0.0 0.0 copy-start
  0.0 0.0 copy-start.1
  0.0 6.3 %shard_map.82 = (f32[768,128]{1,0:T(8,128)}, f32[768,128]{1,0:T(8,128)}) custom-call(f32[1536,128]{1,0:T(8,128)} %bitcast.4, f32[4,128]{1,0:T(4,128)} %wind.1, s32[4,128]{1,0:T(4,128)} %count.1, f32[384]{0:T(512)} %growth.1, s32[768,384]{1,0:T(8,128)} %bitcast.3, s32[512,256]{1,0:T(8,128)} %ocean.3), custom_call_target="tpu_custom_call" | custom-call | flops 6000000000 | bytes 1000 | tf_op jit(solution)/shard_map/pallas_call | solution.py:512
  6.3 2.1 %collective-permute-start = (f32[768,128]{1,0:T(8,128)}, f32[768,128]{1,0:T(8,128)S(1)}, u32[]{:S(2)}, u32[]{:S(2)}) collective-permute-start(f32[768,128]{1,0:T(8,128)} %get-tuple-element.18.east), channel_id=1, source_target_pairs={{0,1},{1,2},{2,3},{3,4},{4,5},{5,6},{6,7},{7,8},{8,9},{9,10},{10,1... | collective-permute-start | bytes 1179656 | tf_op jit(solution)/shard_map/ppermute | solution.py:523
  8.4 9.1 %collective-permute-start.1 = (f32[768,128]{1,0:T(8,128)}, f32[768,128]{1,0:T(8,128)S(1)}, u32[]{:S(2)}, u32[]{:S(2)}) collective-permute-start(f32[768,128]{1,0:T(8,128)} %get-tuple-element.19.west), channel_id=1, source_target_pairs={{0,127},{1,0},{2,1},{3,2},{4,3},{5,4},{6,5},{7,6},{8,7},{9,8},{10,... | collective-permute-start | bytes 1179656 | tf_op jit(solution)/shard_map/ppermute | solution.py:524
  17.5 0.0 copy-done
  17.5 0.0 copy-done.1
  17.5 3.4 %shard_map.83 = (f32[768,128]{1,0:T(8,128)S(1)}, f32[768,128]{1,0:T(8,128)S(1)}, f32[384,128]{1,0:T(8,128)S(1)}, f32[384,128]{1,0:T(8,128)S(1)}, f32[12,256]{1,0:T(8,128)S(1)}) custom-call(f32[16]{0:T(128)S(1)} %copy-done, s32[16]{0:T(128)S(1)} %copy-done.1, s32[512,256]{1,0:T(8,128)} %ocean.3, f32[768,128]{1,0:T(8,128)} %get-tuple-element.18.east, ...), custom_call_target="tpu_custom_call" | custom-call | flops 3000000000 | bytes 1000 | tf_op jit(solution)/shard_map/pallas_call | solution.py:526
  20.9 5.6 %collective-permute-done.refs_0_.east = f32[768,128]{1,0:T(8,128)S(1)} collective-permute-done((f32[768,128]{1,0:T(8,128)}, f32[768,128]{1,0:T(8,128)S(1)}, u32[]{:S(2)}, u32[]{:S(2)}) %collective-permute-start) | collective-permute-done | bytes 393248 | tf_op jit(solution)/shard_map/ppermute | solution.py:523
  26.5 0.0 collective-permute-done.1.west
  26.5 1.4 %shard_map.85 = (f32[384,128]{1,0:T(8,128)S(1)}, f32[384,128]{1,0:T(8,128)S(1)}, f32[2,384,128]{2,1,0:T(8,128)S(1)}) custom-call(f32[16]{0:T(128)S(1)} %copy-done, s32[16]{0:T(128)S(1)} %copy-done.1, f32[12,256]{1,0:T(8,128)S(1)} %get-tuple-element.20.masks_ref, f32[768,128]{1,0:T(8,128)S(1)} %collective-permute-done.refs_0_.east, ...), custom_call_target="tpu_custom_call" | custom-call | flops 1000000000 | bytes 1000 | tf_op jit(solution)/shard_map/pallas_call | solution.py:544
  27.8 1.3 %collective-permute-start.2 = (f32[2,384,128]{2,1,0:T(8,128)S(1)}, f32[2,384,128]{2,1,0:T(8,128)S(1)}, u32[]{:S(2)}, u32[]{:S(2)}) collective-permute-start(f32[2,384,128]{2,1,0:T(8,128)S(1)} %get-tuple-element.29), channel_id=1, source_target_pairs={{0,128},{128,0},{1,129},{129,1},{2,130},{130,2},{3,131},{131,3},{4... | collective-permute-start | bytes 1179656 | tf_op jit(solution)/shard_map/ppermute | solution.py:570
  29.1 1.3 %shard_map.86 = (f32[384,128]{1,0:T(8,128)S(1)}, f32[384,128]{1,0:T(8,128)S(1)}, f32[16,96,128]{2,1,0:T(8,128)}) custom-call(f32[16]{0:T(128)S(1)} %copy-done, s32[16]{0:T(128)S(1)} %copy-done.1, f32[12,256]{1,0:T(8,128)S(1)} %get-tuple-element.20.masks_ref, f32[768,128]{1,0:T(8,128)S(1)} %collective-permute-done.refs_0_.east, ...), custom_call_target="tpu_custom_call" | custom-call | flops 1000000000 | bytes 1000 | tf_op jit(solution)/shard_map/pallas_call | solution.py:544
  30.5 0.0 collective-permute-done.2.cross
  30.5 0.8 %shard_map.87 = f32[16,96,128]{2,1,0:T(8,128)} custom-call(f32[384,128]{1,0:T(8,128)S(1)} %get-tuple-element.27.stage0, f32[384,128]{1,0:T(8,128)S(1)} %get-tuple-element.28.stage1, f32[2,384,128]{2,1,0:T(8,128)S(1)} %collective-permute-done.2.cross, f32[16,96,128]{2,1,0:T(8,128)} %get-tuple-element.30._), custom_call_target="tpu_custom_call", output_to_operand_aliasing={{}: (3, {})} | custom-call | tf_op jit(solution)/shard_map/pallas_call | solution.py:575
  (1 shorter events, 0.0 us)
Async XLA Ops:
  0.0 17.5 %copy-start = (f32[16]{0:T(128)S(1)}, f32[16]{0:T(128)}, u32[]{:S(2)}) copy-start(f32[16]{0:T(128)} %courant_ref.5) | copy-start | bytes 196
  0.0 17.5 %copy-start.1 = (s32[16]{0:T(128)S(1)}, s32[16]{0:T(128)}, u32[]{:S(2)}) copy-start(s32[16]{0:T(128)} %times_ref.5) | copy-start | bytes 196
  6.3 20.2 %collective-permute-start = (f32[768,128]{1,0:T(8,128)}, f32[768,128]{1,0:T(8,128)S(1)}, u32[]{:S(2)}, u32[]{:S(2)}) collective-permute-start(f32[768,128]{1,0:T(8,128)} %get-tuple-element.18.east), channel_id=1, source_target_pairs={{0,1},{1,2},{2,3},{3,4},{4,5},{5,6},{6,7},{7,8},{8,9},{9,10},{10,1... | collective-permute-start | bytes 1179656 | tf_op jit(solution)/shard_map/ppermute | solution.py:523
  8.4 18.1 %collective-permute-start.1 = (f32[768,128]{1,0:T(8,128)}, f32[768,128]{1,0:T(8,128)S(1)}, u32[]{:S(2)}, u32[]{:S(2)}) collective-permute-start(f32[768,128]{1,0:T(8,128)} %get-tuple-element.19.west), channel_id=1, source_target_pairs={{0,127},{1,0},{2,1},{3,2},{4,3},{5,4},{6,5},{7,6},{8,7},{9,8},{10,... | collective-permute-start | bytes 1179656 | tf_op jit(solution)/shard_map/ppermute | solution.py:524
  27.8 2.7 %collective-permute-start.2 = (f32[2,384,128]{2,1,0:T(8,128)S(1)}, f32[2,384,128]{2,1,0:T(8,128)S(1)}, u32[]{:S(2)}, u32[]{:S(2)}) collective-permute-start(f32[2,384,128]{2,1,0:T(8,128)S(1)} %get-tuple-element.29), channel_id=1, source_target_pairs={{0,128},{128,0},{1,129},{129,1},{2,130},{130,2},{3,131},{131,3},{4... | collective-permute-start | bytes 1179656 | tf_op jit(solution)/shard_map/ppermute | solution.py:570

commit v2 on v1

--- a/solution.py
+++ b/solution.py
@@ -219,7 +219,7 @@
         copy.wait()
 
 
-BATCH = (12, 6)
+BATCH = (12, 4)
 
 
 def fine(value, active):

time: 31.4 us -> 31.6 us (level)
  Pallas kernels: 13.1 us -> 13.6 us
  transfers between devices with their start and end apart: 3 -> 3, of which waited for: 1 -> 1; matrix products, arithmetic and copies ran while one was open for 0% -> 0% of each run, Pallas kernels for 15% -> 16%
where the time goes in v2:
time: 31.6 us; the launch traced here: 31.5 us
  Pallas kernels  13.6 us (43%)
  starting transfers between devices  12.5 us (40%)
  waiting for transfers between devices  5.33 us (17%)
    ppermute x1, starting transfers between devices, local(): halo_west = lax.ppermute(west, 'dev', [(i, (i - 1) % n_dev) for i in ring])  9.09 us
    pallas_call x1, Pallas kernels, local(): pl.pallas_call(source_kernel, out_shape=(half_shape, half_shape), in_spec...  6.25 us
    ppermute x1, waiting for transfers between devices, local(): halo_east = lax.ppermute(east, 'dev', [(i, (i + 1) % n_dev) for i in ring])  5.3 us
    pallas_call x1, Pallas kernels, local(): pl.pallas_call(own_kernel, out_shape=(half_shape, half_shape, cross_shape...  3.66 us
    pallas_call x2, Pallas kernels, tail(): pl.pallas_call(kernel, out_shape=outs, in_specs=[SMEM] * 2 + [VMEM] * (1...  2.83 us
    ppermute x1, starting transfers between devices, local(): halo_east = lax.ppermute(east, 'dev', [(i, (i + 1) % n_dev) for i in ring])  2.12 us
    ppermute x1, starting transfers between devices, local(): cross = lax.ppermute(cross, 'hemi', [(0, 1), (1, 0)])  1.31 us
    pallas_call x1, Pallas kernels, local(): pl.pallas_call(join_kernel, out_shape=out_shape, in_specs=[VMEM] * 3 + [H...  0.81 us
  transfers between devices with their start and end apart: 3, of which 1 were waited for; matrix products, arithmetic and copies ran while one was open for 0% of the time, Pallas kernels for 16%

profile of v2, /device:TPU:1, one launch (start us, length us, event | category | flops | bytes accessed | tf_op | source)
XLA Modules:
  0.0 31.5 jit_solution(12682257310707699559)
XLA Ops:
  0.0 0.0 copy-start
  0.0 0.0 copy-start.1
  0.0 6.3 %shard_map.82 = (f32[768,128]{1,0:T(8,128)}, f32[768,128]{1,0:T(8,128)}) custom-call(f32[1536,128]{1,0:T(8,128)} %bitcast.4, f32[4,128]{1,0:T(4,128)} %wind.1, s32[4,128]{1,0:T(4,128)} %count.1, f32[384]{0:T(512)} %growth.1, s32[768,384]{1,0:T(8,128)} %bitcast.3, s32[512,256]{1,0:T(8,128)} %ocean.3), custom_call_target="tpu_custom_call" | custom-call | flops 6000000000 | bytes 1000 | tf_op jit(solution)/shard_map/pallas_call | solution.py:512
  6.3 2.1 %collective-permute-start = (f32[768,128]{1,0:T(8,128)}, f32[768,128]{1,0:T(8,128)S(1)}, u32[]{:S(2)}, u32[]{:S(2)}) collective-permute-start(f32[768,128]{1,0:T(8,128)} %get-tuple-element.18.east), channel_id=1, source_target_pairs={{0,1},{1,2},{2,3},{3,4},{4,5},{5,6},{6,7},{7,8},{8,9},{9,10},{10,1... | collective-permute-start | bytes 1179656 | tf_op jit(solution)/shard_map/ppermute | solution.py:523
  8.4 9.1 %collective-permute-start.1 = (f32[768,128]{1,0:T(8,128)}, f32[768,128]{1,0:T(8,128)S(1)}, u32[]{:S(2)}, u32[]{:S(2)}) collective-permute-start(f32[768,128]{1,0:T(8,128)} %get-tuple-element.19.west), channel_id=1, source_target_pairs={{0,127},{1,0},{2,1},{3,2},{4,3},{5,4},{6,5},{7,6},{8,7},{9,8},{10,... | collective-permute-start | bytes 1179656 | tf_op jit(solution)/shard_map/ppermute | solution.py:524
  17.5 0.0 copy-done
  17.5 0.0 copy-done.1
  17.5 3.7 %shard_map.83 = (f32[768,128]{1,0:T(8,128)S(1)}, f32[768,128]{1,0:T(8,128)S(1)}, f32[384,128]{1,0:T(8,128)S(1)}, f32[384,128]{1,0:T(8,128)S(1)}, f32[12,256]{1,0:T(8,128)S(1)}) custom-call(f32[16]{0:T(128)S(1)} %copy-done, s32[16]{0:T(128)S(1)} %copy-done.1, s32[512,256]{1,0:T(8,128)} %ocean.3, f32[768,128]{1,0:T(8,128)} %get-tuple-element.18.east, ...), custom_call_target="tpu_custom_call" | custom-call | flops 3000000000 | bytes 1000 | tf_op jit(solution)/shard_map/pallas_call | solution.py:526
  21.2 5.3 %collective-permute-done.refs_0_.east = f32[768,128]{1,0:T(8,128)S(1)} collective-permute-done((f32[768,128]{1,0:T(8,128)}, f32[768,128]{1,0:T(8,128)S(1)}, u32[]{:S(2)}, u32[]{:S(2)}) %collective-permute-start) | collective-permute-done | bytes 393248 | tf_op jit(solution)/shard_map/ppermute | solution.py:523
  26.5 0.0 collective-permute-done.1.west
  26.5 1.5 %shard_map.85 = (f32[384,128]{1,0:T(8,128)S(1)}, f32[384,128]{1,0:T(8,128)S(1)}, f32[2,384,128]{2,1,0:T(8,128)S(1)}) custom-call(f32[16]{0:T(128)S(1)} %copy-done, s32[16]{0:T(128)S(1)} %copy-done.1, f32[12,256]{1,0:T(8,128)S(1)} %get-tuple-element.20.masks_ref, f32[768,128]{1,0:T(8,128)S(1)} %collective-permute-done.refs_0_.east, ...), custom_call_target="tpu_custom_call" | custom-call | flops 1000000000 | bytes 1000 | tf_op jit(solution)/shard_map/pallas_call | solution.py:544
  28.0 1.3 %collective-permute-start.2 = (f32[2,384,128]{2,1,0:T(8,128)S(1)}, f32[2,384,128]{2,1,0:T(8,128)S(1)}, u32[]{:S(2)}, u32[]{:S(2)}) collective-permute-start(f32[2,384,128]{2,1,0:T(8,128)S(1)} %get-tuple-element.29), channel_id=1, source_target_pairs={{0,128},{128,0},{1,129},{129,1},{2,130},{130,2},{3,131},{131,3},{4... | collective-permute-start | bytes 1179656 | tf_op jit(solution)/shard_map/ppermute | solution.py:570
  29.3 1.3 %shard_map.86 = (f32[384,128]{1,0:T(8,128)S(1)}, f32[384,128]{1,0:T(8,128)S(1)}, f32[16,96,128]{2,1,0:T(8,128)}) custom-call(f32[16]{0:T(128)S(1)} %copy-done, s32[16]{0:T(128)S(1)} %copy-done.1, f32[12,256]{1,0:T(8,128)S(1)} %get-tuple-element.20.masks_ref, f32[768,128]{1,0:T(8,128)S(1)} %collective-permute-done.refs_0_.east, ...), custom_call_target="tpu_custom_call" | custom-call | flops 1000000000 | bytes 1000 | tf_op jit(solution)/shard_map/pallas_call | solution.py:544
  30.6 0.0 collective-permute-done.2.cross
  30.6 0.8 %shard_map.87 = f32[16,96,128]{2,1,0:T(8,128)} custom-call(f32[384,128]{1,0:T(8,128)S(1)} %get-tuple-element.27.stage0, f32[384,128]{1,0:T(8,128)S(1)} %get-tuple-element.28.stage1, f32[2,384,128]{2,1,0:T(8,128)S(1)} %collective-permute-done.2.cross, f32[16,96,128]{2,1,0:T(8,128)} %get-tuple-element.30._), custom_call_target="tpu_custom_call", output_to_operand_aliasing={{}: (3, {})} | custom-call | tf_op jit(solution)/shard_map/pallas_call | solution.py:575
  (1 shorter events, 0.0 us)
Async XLA Ops:
  0.0 17.5 %copy-start = (f32[16]{0:T(128)S(1)}, f32[16]{0:T(128)}, u32[]{:S(2)}) copy-start(f32[16]{0:T(128)} %courant_ref.5) | copy-start | bytes 196
  0.0 17.5 %copy-start.1 = (s32[16]{0:T(128)S(1)}, s32[16]{0:T(128)}, u32[]{:S(2)}) copy-start(s32[16]{0:T(128)} %times_ref.5) | copy-start | bytes 196
  6.3 20.2 %collective-permute-start = (f32[768,128]{1,0:T(8,128)}, f32[768,128]{1,0:T(8,128)S(1)}, u32[]{:S(2)}, u32[]{:S(2)}) collective-permute-start(f32[768,128]{1,0:T(8,128)} %get-tuple-element.18.east), channel_id=1, source_target_pairs={{0,1},{1,2},{2,3},{3,4},{4,5},{5,6},{6,7},{7,8},{8,9},{9,10},{10,1... | collective-permute-start | bytes 1179656 | tf_op jit(solution)/shard_map/ppermute | solution.py:523
  8.4 18.1 %collective-permute-start.1 = (f32[768,128]{1,0:T(8,128)}, f32[768,128]{1,0:T(8,128)S(1)}, u32[]{:S(2)}, u32[]{:S(2)}) collective-permute-start(f32[768,128]{1,0:T(8,128)} %get-tuple-element.19.west), channel_id=1, source_target_pairs={{0,127},{1,0},{2,1},{3,2},{4,3},{5,4},{6,5},{7,6},{8,7},{9,8},{10,... | collective-permute-start | bytes 1179656 | tf_op jit(solution)/shard_map/ppermute | solution.py:524
  28.0 2.7 %collective-permute-start.2 = (f32[2,384,128]{2,1,0:T(8,128)S(1)}, f32[2,384,128]{2,1,0:T(8,128)S(1)}, u32[]{:S(2)}, u32[]{:S(2)}) collective-permute-start(f32[2,384,128]{2,1,0:T(8,128)S(1)} %get-tuple-element.29), channel_id=1, source_target_pairs={{0,128},{128,0},{1,129},{129,1},{2,130},{130,2},{3,131},{131,3},{4... | collective-permute-start | bytes 1179656 | tf_op jit(solution)/shard_map/ppermute | solution.py:570
